TPU v7x, 1024 devices: a whole 4x8x16 slice. The times are simulated.
1024 devices in a mesh: dp: 16 (over z), expert: 64 (over y, x, core).
Axes of the slice: x: 4, y: 8, z: 16, core: 2. Of those that a mesh axis runs over, the one named last changes fastest.
Arguments:
- tokens: bfloat16 [8192, 3584], P('expert', 'dp'), may hold values from -6 to 6
- cotangent: bfloat16 [8192, 3584], P('expert', 'dp'), may hold values from -1.1953125 to 1.1953125
- expert_ids: int32 [8192, 2], P('expert'), may hold values from 0 to 63, all different within a row; in each aligned block of 128 rows (0 to 127, 128 to 255, ...) at most 5 rows name the same one
- combine: float32 [8192, 2], P('expert'), may hold values from 0.2 to 1
- w_up: bfloat16 [64, 3584, 2432], P('expert', 'dp'), may hold values from -0.09375 to 0.09375
- w_down: bfloat16 [64, 2432, 3584], P('expert', None, 'dp'), may hold values from -0.125 to 0.125
Outputs:
- layer_out: bfloat16 [8192, 3584], P('expert', 'dp')
- input_grad: bfloat16 [8192, 3584], P('expert', 'dp')
- combine_grad: float32 [8192, 2], P('expert')
- down_grad: bfloat16 [64, 2432, 3584], P('expert', None, 'dp')
Inputs may be any that keep to these rules, and one draw needn't show every extreme that they name: `expert_ids`: the two ids of a token differ. Among the 256 ids of one index s of expert (tokens s * 128 to (s + 1) * 128 - 1), no expert appears more than 5 times, and some expert appears exactly 5 times.
All inputs are finite; a program needn't handle non-finite values.
Results may differ from a plain program's by a relative error of at most 0.029.
Values may be sent and summed in bfloat16 or wider, within the bound.
No kernel may reach another device: no remote copies, remote signals or barrier semaphores. Data moves between devices by JAX's collectives and lax.ppermute only.
A program may use at most 32 MiB of HBM per device.

v0:
```python
import functools

import jax
import jax.numpy as jnp
from jax import lax
from jax.experimental import pallas as pl
from jax.experimental.pallas import tpu as pltpu
from jax.sharding import PartitionSpec as P

CAP = 5
PAD = 8
TILE = 128
F32 = jnp.float32
BF16 = jnp.bfloat16
VMEM = pl.BlockSpec(memory_space=pltpu.VMEM)
HBM = pl.BlockSpec(memory_space=pltpu.HBM)
NN = (((1,), (0,)), ((), ()))
NT = (((1,), (1,)), ((), ()))
TN = (((0,), (0,)), ((), ()))


def mm(a, b, dims):
    return lax.dot_general(a, b, dims, preferred_element_type=F32)


def halves(block):
    half = block.shape[0] // 2
    zeros = jnp.zeros((TILE - half, block.shape[1]), block.dtype)
    return jnp.concatenate([block[:half], zeros, block[half:], zeros], axis=0)


def iota(shape, dim):
    return lax.broadcasted_iota(jnp.int32, shape, dim)


def ones_at(mask):
    return jnp.where(mask, 1.0, 0.0).astype(BF16)


def call(kernel, out_shape, out_specs, args, in_specs, scratch=(), limit=60):
    return pl.pallas_call(
        kernel,
        out_shape=out_shape,
        in_specs=in_specs,
        out_specs=out_specs,
        scratch_shapes=list(scratch),
        compiler_params=pltpu.CompilerParams(vmem_limit_bytes=limit * 1024 * 1024),
    )(*args)


def load(pairs, sems):
    copies = [pltpu.make_async_copy(src, dst, sems.at[i]) for i, (src, dst) in enumerate(pairs)]
    for copy in copies:
        copy.start()
    return copies


def dispatch_kernel(ids_hbm, comb_hbm, tok_hbm, cot_hbm, send_ref, disp_ref, ids_ref, comb_ref, tok_ref, cot_ref, sems):
    copies = load(((ids_hbm, ids_ref), (comb_hbm, comb_ref), (tok_hbm, tok_ref), (cot_hbm, cot_ref)), sems)
    rows, toks = send_ref.shape[0], tok_ref.shape[1]
    row = iota((rows, toks), 0)
    expert, slot = row >> 3, row & 7
    earlier = ones_at(iota((toks, toks), 0) < iota((toks, toks), 1))
    copies[0].wait()
    first = expert == ids_ref[0:1, :]
    second = expert == ids_ref[1:2, :]
    chosen = jnp.where(first | second, 1.0, 0.0)
    before = mm(chosen.astype(BF16), earlier, NN).astype(jnp.int32)
    here = [
        jnp.where(before == jnp.where(slot < CAP, slot, jnp.where(slot - shift < CAP, slot - shift, -1)), chosen, 0.0)
        for shift in (5, 2)
    ]
    copies[1].wait()
    weight = jnp.where(first, comb_ref[0:1, :], comb_ref[1:2, :])
    weights = [jnp.sum(h * weight, axis=1, keepdims=True) for h in here]
    picks = [h.astype(BF16) for h in here]
    disp_ref[:, :toks] = picks[0]
    disp_ref[:, toks:] = picks[1]
    copies[2].wait()
    copies[3].wait()
    x, g = halves(tok_ref[...]), halves(cot_ref[...])
    low = iota((rows, TILE), 0) & 7 < CAP
    for i in range(2):
        source = jnp.concatenate([x[TILE * i : TILE * i + TILE], g[TILE:]], axis=0)
        both = mm(picks[i], source, NT)
        send_ref[:, TILE * i : TILE * i + TILE] = jnp.where(low, both[:, :TILE], weights[i] * both[:, TILE:]).astype(BF16)
    send_ref[:, 2 * TILE :] = (weights[0] * mm(picks[0], g[:TILE], NT)).astype(BF16)


def spans(hidden):
    cut = (hidden // 2 + 127) // 128 * 128
    return (0, cut), (cut, hidden)


def pieces_of(refs, kept, hidden):
    places = [(slice(r, r + 16), slice(*span)) for r in range(0, kept, 16) for span in spans(hidden)]
    return [(ref, *place) for ref, place in zip(refs, places, strict=True)]


def up_kernel(count, recv_ref, up_hbm, down_hbm, g_ref, *refs):
    outs, (term_ref, up_ref, down_ref, in_sems, out_sems) = refs[: 2 * count], refs[2 * count :]
    copies = load(((up_hbm, up_ref), (down_hbm, down_ref)), in_sems)
    feat, hidden = up_ref.shape
    half = feat // 2
    kept, padded = g_ref.shape[0], recv_ref.shape[0]
    row = iota((kept, padded), 0)
    source = (row * 13108) >> 16
    slot = row - source * CAP
    at = iota((kept, padded), 1) - source * PAD
    main = mm(ones_at(at == slot), recv_ref[...], NN)
    extra = mm(ones_at(at == jnp.where(slot < 3, slot + 5, padded)), recv_ref[:, :TILE], NN)
    extra += mm(ones_at(at == jnp.where(slot < 3, padded, slot + 2)), recv_ref[:, TILE : 2 * TILE], NN)
    x_rows = jnp.concatenate([main[:, :half], main[:, TILE : TILE + half]], axis=1).astype(BF16)
    g_rows = jnp.concatenate([main[:, 2 * TILE : 2 * TILE + half], extra[:, :half]], axis=1).astype(BF16)
    g_ref[...] = g_rows
    started = []
    for k, (rows, w_ref) in enumerate(((x_rows, up_ref), (g_rows, down_ref))):
        copies[k].wait()
        for at in range(0, hidden, 256):
            cols = slice(at, min(at + 256, hidden))
            term_ref[k, :, cols] = mm(rows, w_ref[:, cols], NN).astype(BF16)
        for i, (out, r, c) in enumerate(pieces_of(outs[k * count : (k + 1) * count], kept, hidden)):
            copy = pltpu.make_async_copy(term_ref.at[k, r, c], out, out_sems.at[k * count + i])
            copy.start()
            started.append(copy)
    for copy in started:
        copy.wait()


def down_kernel(count, *refs):
    sums, (up_hbm, down_hbm) = refs[: 2 * count], refs[2 * count : 2 * count + 2]
    send_ref, act_hbm, sum_ref, act_ref, dhid_ref, dots_ref, up_ref, down_ref, sems, w_sems = refs[2 * count + 2 :]
    kept, hidden = act_ref.shape
    padded, feat = send_ref.shape[0], up_ref.shape[0]
    half = feat // 2
    hid = pieces_of(sums[:count], kept, hidden)
    dact = pieces_of(sums[count:], kept, hidden)
    waits = []
    for i in range(count):
        for k, (ref, r, c) in enumerate((hid[i], dact[i])):
            copy = pltpu.make_async_copy(ref, sum_ref.at[k, r, c], sems.at[k * count + i])
            copy.start()
            waits.append(copy)
    copies = load(((up_hbm, up_ref), (down_hbm, down_ref)), w_sems)
    for i in range(0, count, 2):
        for copy in waits[2 * i : 2 * i + 4]:
            copy.wait()
        rows = hid[i][1]
        h = sum_ref[0, rows, :].astype(F32)
        d = sum_ref[1, rows, :].astype(F32)
        s = 1.0 / (1.0 + jnp.exp(-h))
        act = (h * s).astype(BF16)
        act_ref[rows, :] = act
        dhid_ref[rows, :] = (d * (s * (1.0 + h * (1.0 - s)))).astype(BF16)
        dots_ref[rows, :] = jnp.broadcast_to(jnp.sum(act.astype(F32) * d, axis=1, keepdims=True), (16, TILE))
    act_copy = pltpu.make_async_copy(act_ref, act_hbm, w_sems.at[2])
    act_copy.start()
    row = iota((padded, kept), 0)
    slot = row & 7
    at = iota((padded, kept), 1) - (row >> 3) * CAP
    base = ones_at((at == slot) & (slot < CAP))
    copies[1].wait()
    y = mm(act_ref[...], halves(down_ref[...]), NT).astype(BF16)
    dots = dots_ref[...]
    high = dots.astype(BF16).astype(F32)
    lane = iota((kept, TILE), 1)
    low = jnp.where(lane == half, high, jnp.where(lane == half + 1, dots - high, y[:, :TILE].astype(F32))).astype(BF16)
    copies[0].wait()
    dx = mm(dhid_ref[...], halves(up_ref[...]), NT).astype(BF16)
    for i, (part, shift) in enumerate(((low, 5), (y[:, TILE:], 2))):
        lift = ones_at((slot >= CAP) & (slot - shift < (3 if i == 0 else CAP)) & (at == slot - shift))
        tile = mm(base, part, NN) + mm(lift, dx[:, TILE:], NN)
        send_ref[:, TILE * i : TILE * i + TILE] = tile.astype(BF16)
    send_ref[:, 2 * TILE :] = mm(base, dx[:, :TILE], NN).astype(BF16)
    act_copy.wait()


def grad_kernel(g_ref, act_ref, out_ref):
    hidden = act_ref.shape[1]
    for at in range(0, hidden, 256):
        cols = slice(at, min(at + 256, hidden))
        out_ref[:, cols] = mm(g_ref[...], act_ref[:, cols], TN).astype(BF16)


def combine_kernel(recv_ref, disp_ref, ids_ref, comb_ref, tok_ref, cot_ref, out_ref, dx_ref, grad_ref):
    rows = recv_ref.shape[0]
    feat, toks = tok_ref.shape
    half = feat // 2
    row = iota((rows, toks), 0)
    expert, main = row >> 3, row & 7 < CAP
    pick = disp_ref[:, :toks].astype(F32)
    shift = disp_ref[:, toks:].astype(F32)
    base = jnp.where(main, pick, 0.0)
    total = [tok_ref[:half, :].astype(F32), tok_ref[half:, :].astype(F32)]
    for k in range(2):
        mine = jnp.where(expert == ids_ref[k : k + 1, :], base, 0.0).astype(BF16)
        y = mm(recv_ref[:, : 2 * TILE], mine, TN)
        weight = comb_ref[k : k + 1, :]
        total = [total[i] + weight * y[TILE * i : TILE * i + half] for i in range(2)]
        grad_ref[k : k + 1, :] = (y[half : half + 1] + y[half + 1 : half + 2]) / weight
    out_ref[:half, :] = total[0].astype(BF16)
    out_ref[half:, :] = total[1].astype(BF16)
    dx_low = mm(recv_ref[:, 2 * TILE :], base.astype(BF16), TN)
    dx_high = mm(recv_ref[:, :TILE], jnp.where(main, 0.0, pick).astype(BF16), TN)
    dx_high += mm(recv_ref[:, TILE : 2 * TILE], jnp.where(main, 0.0, shift).astype(BF16), TN)
    dx_ref[:half, :] = (cot_ref[:half, :].astype(F32) + dx_low[:half]).astype(BF16)
    dx_ref[half:, :] = (cot_ref[half:, :].astype(F32) + dx_high[:half]).astype(BF16)


def exchange(rows, groups):
    parts = rows.reshape(groups, PAD, 3 * TILE)
    parts = lax.all_to_all(parts, "expert", split_axis=0, concat_axis=0, tiled=True)
    return parts.reshape(groups * PAD, 3 * TILE)


def body(tokens, cotangent, expert_ids, combine, w_up, w_down):
    toks, feat = tokens.shape
    groups = lax.axis_size("expert")
    hidden = w_up.shape[2]
    kept, padded = groups * CAP, groups * PAD
    count = kept // 16 * 2
    shape = jax.ShapeDtypeStruct
    dma = pltpu.SemaphoreType.DMA
    tok, cot, ids, comb = tokens.T, cotangent.T, expert_ids.T, combine.T
    up, down = w_up[0], w_down[0].T
    weights = [pltpu.VMEM((feat, hidden), BF16)] * 2

    send, disp = call(
        dispatch_kernel,
        (shape((padded, 3 * TILE), BF16), shape((padded, 2 * toks), BF16)),
        (VMEM, VMEM),
        (ids, comb, tok, cot),
        [HBM] * 4,
        [pltpu.VMEM(a.shape, a.dtype) for a in (ids, comb, tok, cot)] + [dma((4,))],
    )
    recv = exchange(send, groups)
    pieces = tuple(shape((16, b - a), BF16) for _ in range(kept // 16) for a, b in spans(hidden))
    g_rows, *terms = call(
        functools.partial(up_kernel, count),
        (shape((kept, feat), BF16),) + 2 * pieces,
        (VMEM,) + (HBM,) * (2 * count),
        (recv, up, down),
        [VMEM, HBM, HBM],
        [pltpu.VMEM((2, kept, hidden), BF16), *weights, dma((2,)), dma((2 * count,))],
    )
    sums = lax.psum(tuple(terms), "dp")
    send_back, act = call(
        functools.partial(down_kernel, count),
        (shape((padded, 3 * TILE), BF16), shape((kept, hidden), BF16)),
        (VMEM, HBM),
        (*sums, up, down),
        [HBM] * (2 * count + 2),
        [
            pltpu.VMEM((2, kept, hidden), BF16),
            pltpu.VMEM((kept, hidden), BF16),
            pltpu.VMEM((kept, hidden), BF16),
            pltpu.VMEM((kept, TILE), F32),
            *weights,
            dma((2 * count,)),
            dma((3,)),
        ],
    )
    back = exchange(send_back, groups)
    down_grad = call(grad_kernel, shape((feat, hidden), BF16), VMEM, (g_rows, act), [VMEM] * 2)
    layer_out, input_grad, combine_grad = call(
        combine_kernel,
        (shape((feat, toks), BF16), shape((feat, toks), BF16), shape((2, toks), F32)),
        (VMEM,) * 3,
        (back, disp, ids, comb, tok, cot),
        [VMEM] * 6,
        limit=8,
    )
    return layer_out.T, input_grad.T, combine_grad.T, down_grad.T[None]


def solution(mesh):
    in_specs = (
        P("expert", "dp"),
        P("expert", "dp"),
        P("expert", None),
        P("expert", None),
        P("expert", "dp", None),
        P("expert", None, "dp"),
    )
    out_specs = (P("expert", "dp"), P("expert", "dp"), P("expert", None), P("expert", None, "dp"))
    return jax.shard_map(body, mesh=mesh, in_specs=in_specs, out_specs=out_specs, check_vma=False)
```

profile of v0, /device:TPU:1, one launch (start us, length us, event | category | flops | bytes accessed | tf_op | source)
XLA Modules:
  0.0 160.4 jit_solution(11545909842075384216)
XLA Ops:
  0.6 2.3 %shard_map.93 = (bf16[512,384]{1,0:T(8,128)(2,1)}, bf16[512,256]{1,0:T(8,128)(2,1)}) custom-call(s32[2,128]{1,0:T(2,128)} %bitcast.23, f32[2,128]{1,0:T(2,128)} %bitcast.25, bf16[224,128]{1,0:T(8,128)(2,1)} %bitcast.19, bf16[224,128]{1,0:T(8,128)(2,1)} %bitcast.21), custom_call_target="tpu_custom_call" | custom-call | tf_op jit(solution)/shard_map/pallas_call | solution.py:41
  3.0 34.1 %all_to_all.10 = bf16[64,8,384]{2,1,0:T(8,128)(2,1)} all-to-all(bf16[64,8,384]{2,1,0:T(8,128)(2,1)} %bitcast.34), channel_id=1, replica_groups=mesh['dp'=16,'expert'=64] {'expert'}, dimensions={0} | all-to-all | bytes 786432 | tf_op jit(solution)/shard_map/all_to_all | solution.py:212
  37.1 6.1 %shard_map.94 = (bf16[320,224]{1,0:T(8,128)(2,1)}, bf16[16,1280]{1,0:T(8,128)(2,1)}, bf16[16,1152]{1,0:T(8,128)(2,1)}, bf16[16,1280]{1,0:T(8,128)(2,1)}, bf16[16...) custom-call(bf16[512,384]{1,0:T(8,128)(2,1)} %bitcast.31, ...), custom_call_target="tpu_custom_call" | custom-call | tf_op jit(solution)/shard_map/pallas_call | solution.py:41
  43.2 78.4 %all-reduce.2 = (bf16[16,1280]{1,0:T(8,128)(2,1)}, bf16[16,1152]{1,0:T(8,128)(2,1)}, bf16[16,1280]{1,0:T(8,128)(2,1)}, bf16[16,1152]{1,0:T(8,128)(2,1)}, bf16[16...) all-reduce(bf16[16,1280]{1,0:T(8,128)(2,1)} %get-tuple-element.93, ...), channel_id=1, replica_groups=mesh['dp'=16,'expert'=64] {'dp'}, use_global_device_ids=true, to_apply=%region_0.0 | all-reduce | flops 1556480 | bytes 6225920 | tf_op jit(solution)/shard_map/psum | solution.py:246
  121.6 8.1 %shard_map.95 = (bf16[512,384]{1,0:T(8,128)(2,1)}, bf16[320,2432]{1,0:T(8,128)(2,1)}) custom-call(bf16[16,1280]{1,0:T(8,128)(2,1)} %get-tuple-element.180.refs_0_, bf16[16,1152]{1,0:T(8,128)(2,1)} %get-tuple-element.181.refs_1_, bf16[16,1280]{1,0:T(8,128)(2,1)} %get-tuple-element.182.refs_2_, bf16[16,1152]{1,0:T(8,128)(2,1)} %get-tuple-element.183.refs_3_, ...), custom_call_target="tpu_custom_call" | custom-call | tf_op jit(solution)/shard_map/pallas_call | solution.py:41
  129.7 14.5 %all-to-all-start.1 = ((bf16[64,8,384]{2,1,0:T(8,128)(2,1)}), bf16[64,8,384]{2,1,0:T(8,128)(2,1)S(1)}, u32[]{:S(2)}, u32[]{:S(2)}) async-start(bf16[64,8,384]{2,1,0:T(8,128)(2,1)} %bitcast.33), calls=%async_computation.1 | async-start | bytes 786432 | tf_op jit(solution)/shard_map/all_to_all | solution.py:212
  144.2 0.0 copy-start
  144.3 0.0 copy-start.1
  144.3 0.0 copy-start.2
  144.3 0.0 copy-start.3
  144.3 0.0 copy-start.4
  144.3 3.3 %shard_map.97 = bf16[224,2432]{1,0:T(8,128)(2,1)} custom-call(bf16[320,224]{1,0:T(8,128)(2,1)} %get-tuple-element.178.g_ref, bf16[320,2432]{1,0:T(8,128)(2,1)} %get-tuple-element.179.act_ref), custom_call_target="tpu_custom_call" | custom-call | tf_op jit(solution)/shard_map/pallas_call | solution.py:41
  147.6 11.7 %all-to-all-done.1 = bf16[64,8,384]{2,1,0:T(8,128)(2,1)S(1)} async-done(((bf16[64,8,384]{2,1,0:T(8,128)(2,1)}), bf16[64,8,384]{2,1,0:T(8,128)(2,1)S(1)}, u32[]{:S(2)}, u32[]{:S(2)}) %all-to-all-start.1) | async-done | bytes 393248 | tf_op jit(solution)/shard_map/all_to_all | solution.py:212
  159.3 0.0 copy-done
  159.3 0.0 copy-done.1
  159.3 0.0 copy-done.2
  159.3 0.0 copy-done.3
  159.3 0.0 copy-done.4
  159.3 1.1 shard_map.96
Async XLA Ops:
  129.7 29.6 %all-to-all-start.1 = ((bf16[64,8,384]{2,1,0:T(8,128)(2,1)}), bf16[64,8,384]{2,1,0:T(8,128)(2,1)S(1)}, u32[]{:S(2)}, u32[]{:S(2)}) async-start(bf16[64,8,384]{2,1,0:T(8,128)(2,1)} %bitcast.33), calls=%async_computation.1 | async-start | bytes 786432 | tf_op jit(solution)/shard_map/all_to_all | solution.py:212
  144.2 15.1 %copy-start = (bf16[512,256]{1,0:T(8,128)(2,1)S(1)}, bf16[512,256]{1,0:T(8,128)(2,1)}, u32[]{:S(2)}) copy-start(bf16[512,256]{1,0:T(8,128)(2,1)} %get-tuple-element.174.disp_ref) | copy-start | bytes 786436
  144.3 15.1 %copy-start.1 = (bf16[128,224]{0,1:T(8,128)(2,1)S(1)}, bf16[128,224]{0,1:T(8,128)(2,1)}, u32[]{:S(2)}) copy-start(bf16[128,224]{0,1:T(8,128)(2,1)} %param.6) | copy-start | bytes 172036
  144.3 15.0 %copy-start.2 = (bf16[128,224]{0,1:T(8,128)(2,1)S(1)}, bf16[128,224]{0,1:T(8,128)(2,1)}, u32[]{:S(2)}) copy-start(bf16[128,224]{0,1:T(8,128)(2,1)} %param.7) | copy-start | bytes 172036
  144.3 15.0 %copy-start.3 = (s32[128,2]{0,1:T(2,128)S(1)}, s32[128,2]{0,1:T(2,128)}, u32[]{:S(2)}) copy-start(s32[128,2]{0,1:T(2,128)} %param.8) | copy-start | bytes 3076
  144.3 15.0 %copy-start.4 = (f32[128,2]{0,1:T(2,128)S(1)}, f32[128,2]{0,1:T(2,128)}, u32[]{:S(2)}) copy-start(f32[128,2]{0,1:T(2,128)} %param.9) | copy-start | bytes 3076
where the time goes:
time: 161 us; the launch traced here: 160 us
  blocking collectives  113 us (70%)
  Pallas kernels  20.9 us (13%)
  starting transfers between devices  14.5 us (9%)
  waiting for transfers between devices  11.7 us (7%)
    psum x1, blocking collectives, body(): sums = lax.psum(tuple(terms), 'dp')  78.4 us
    all_to_all x1, blocking collectives, exchange(): lax.all_to_all(parts, 'expert', split_axis=0, concat_axis=0, tiled=True)  34.1 us
    pallas_call x5, Pallas kernels, call(): pl.pallas_call(kernel, out_shape=out_shape, in_specs=in_specs, out_specs=...  20.9 us
    all_to_all x1, starting transfers between devices, exchange(): lax.all_to_all(parts, 'expert', split_axis=0, concat_axis=0, tiled=True)  14.5 us
    all_to_all x1, waiting for transfers between devices, exchange(): lax.all_to_all(parts, 'expert', split_axis=0, concat_axis=0, tiled=True)  11.7 us
  transfers between devices with their start and end apart: 1, of which 1 were waited for; matrix products, arithmetic and copies ran while one was open for 0% of the time, Pallas kernels for 2%

commit v1 on v0

--- a/solution.py
+++ b/solution.py
@@ -55,7 +55,15 @@
     return copies
 
 
-def dispatch_kernel(ids_hbm, comb_hbm, tok_hbm, cot_hbm, send_ref, disp_ref, ids_ref, comb_ref, tok_ref, cot_ref, sems):
+def ship(src_ref, dst_ref, i, sem):
+    tile = slice(TILE * i, TILE * i + TILE)
+    copy = pltpu.make_async_copy(src_ref.at[:, tile], dst_ref.at[:, tile], sem)
+    copy.start()
+    return copy
+
+
+def dispatch_kernel(ids_hbm, comb_hbm, tok_hbm, cot_hbm, send_hbm, disp_hbm, *scratch):
+    ids_ref, comb_ref, tok_ref, cot_ref, send_ref, disp_ref, sems, out_sems = scratch
     copies = load(((ids_hbm, ids_ref), (comb_hbm, comb_ref), (tok_hbm, tok_ref), (cot_hbm, cot_ref)), sems)
     rows, toks = send_ref.shape[0], tok_ref.shape[1]
     row = iota((rows, toks), 0)
@@ -76,6 +84,8 @@
     picks = [h.astype(BF16) for h in here]
     disp_ref[:, :toks] = picks[0]
     disp_ref[:, toks:] = picks[1]
+    started = [pltpu.make_async_copy(disp_ref, disp_hbm, out_sems.at[3])]
+    started[0].start()
     copies[2].wait()
     copies[3].wait()
     x, g = halves(tok_ref[...]), halves(cot_ref[...])
@@ -84,7 +94,11 @@
         source = jnp.concatenate([x[TILE * i : TILE * i + TILE], g[TILE:]], axis=0)
         both = mm(picks[i], source, NT)
         send_ref[:, TILE * i : TILE * i + TILE] = jnp.where(low, both[:, :TILE], weights[i] * both[:, TILE:]).astype(BF16)
+        started.append(ship(send_ref, send_hbm, i, out_sems.at[i]))
     send_ref[:, 2 * TILE :] = (weights[0] * mm(picks[0], g[:TILE], NT)).astype(BF16)
+    started.append(ship(send_ref, send_hbm, 2, out_sems.at[2]))
+    for copy in started:
+        copy.wait()
 
 
 def spans(hidden):
@@ -92,14 +106,13 @@
     return (0, cut), (cut, hidden)
 
 
-def pieces_of(refs, kept, hidden):
-    places = [(slice(r, r + 16), slice(*span)) for r in range(0, kept, 16) for span in spans(hidden)]
-    return [(ref, *place) for ref, place in zip(refs, places, strict=True)]
-
-
-def up_kernel(count, recv_ref, up_hbm, down_hbm, g_ref, *refs):
-    outs, (term_ref, up_ref, down_ref, in_sems, out_sems) = refs[: 2 * count], refs[2 * count :]
-    copies = load(((up_hbm, up_ref), (down_hbm, down_ref)), in_sems)
+def places(kept, hidden):
+    return [(slice(r, r + 16), slice(*span)) for r in range(0, kept, 16) for span in spans(hidden)]
+
+
+def up_kernel(count, recv_hbm, up_hbm, down_hbm, g_hbm, *refs):
+    outs, (term_ref, recv_ref, g_ref, up_ref, down_ref, in_sems, out_sems) = refs[: 2 * count], refs[2 * count :]
+    copies = load(((up_hbm, up_ref), (down_hbm, down_ref), (recv_hbm, recv_ref)), in_sems)
     feat, hidden = up_ref.shape
     half = feat // 2
     kept, padded = g_ref.shape[0], recv_ref.shape[0]
@@ -107,20 +120,22 @@
     source = (row * 13108) >> 16
     slot = row - source * CAP
     at = iota((kept, padded), 1) - source * PAD
+    copies[2].wait()
     main = mm(ones_at(at == slot), recv_ref[...], NN)
     extra = mm(ones_at(at == jnp.where(slot < 3, slot + 5, padded)), recv_ref[:, :TILE], NN)
     extra += mm(ones_at(at == jnp.where(slot < 3, padded, slot + 2)), recv_ref[:, TILE : 2 * TILE], NN)
     x_rows = jnp.concatenate([main[:, :half], main[:, TILE : TILE + half]], axis=1).astype(BF16)
     g_rows = jnp.concatenate([main[:, 2 * TILE : 2 * TILE + half], extra[:, :half]], axis=1).astype(BF16)
     g_ref[...] = g_rows
-    started = []
+    started = [pltpu.make_async_copy(g_ref, g_hbm, out_sems.at[2 * count])]
+    started[0].start()
     for k, (rows, w_ref) in enumerate(((x_rows, up_ref), (g_rows, down_ref))):
         copies[k].wait()
         for at in range(0, hidden, 256):
             cols = slice(at, min(at + 256, hidden))
             term_ref[k, :, cols] = mm(rows, w_ref[:, cols], NN).astype(BF16)
-        for i, (out, r, c) in enumerate(pieces_of(outs[k * count : (k + 1) * count], kept, hidden)):
-            copy = pltpu.make_async_copy(term_ref.at[k, r, c], out, out_sems.at[k * count + i])
+        for i, (r, c) in enumerate(places(kept, hidden), k * count):
+            copy = pltpu.make_async_copy(term_ref.at[k, r, c], outs[i], out_sems.at[i])
             copy.start()
             started.append(copy)
     for copy in started:
@@ -129,23 +144,21 @@
 
 def down_kernel(count, *refs):
     sums, (up_hbm, down_hbm) = refs[: 2 * count], refs[2 * count : 2 * count + 2]
-    send_ref, act_hbm, sum_ref, act_ref, dhid_ref, dots_ref, up_ref, down_ref, sems, w_sems = refs[2 * count + 2 :]
+    send_hbm, act_hbm, sum_ref, act_ref, dhid_ref, dots_ref, up_ref, down_ref, send_ref, sems, w_sems = refs[2 * count + 2 :]
     kept, hidden = act_ref.shape
     padded, feat = send_ref.shape[0], up_ref.shape[0]
     half = feat // 2
-    hid = pieces_of(sums[:count], kept, hidden)
-    dact = pieces_of(sums[count:], kept, hidden)
-    waits = []
-    for i in range(count):
-        for k, (ref, r, c) in enumerate((hid[i], dact[i])):
-            copy = pltpu.make_async_copy(ref, sum_ref.at[k, r, c], sems.at[k * count + i])
+    waits = {}
+    for i, (r, c) in enumerate(places(kept, hidden)):
+        for k in range(2):
+            copy = pltpu.make_async_copy(sums[k * count + i], sum_ref.at[k, r, c], sems.at[k * count + i])
             copy.start()
-            waits.append(copy)
+            waits.setdefault(r.start, []).append(copy)
     copies = load(((up_hbm, up_ref), (down_hbm, down_ref)), w_sems)
-    for i in range(0, count, 2):
-        for copy in waits[2 * i : 2 * i + 4]:
+    for first in range(0, kept, 16):
+        for copy in waits[first]:
             copy.wait()
-        rows = hid[i][1]
+        rows = slice(first, first + 16)
         h = sum_ref[0, rows, :].astype(F32)
         d = sum_ref[1, rows, :].astype(F32)
         s = 1.0 / (1.0 + jnp.exp(-h))
@@ -167,12 +180,15 @@
     low = jnp.where(lane == half, high, jnp.where(lane == half + 1, dots - high, y[:, :TILE].astype(F32))).astype(BF16)
     copies[0].wait()
     dx = mm(dhid_ref[...], halves(up_ref[...]), NT).astype(BF16)
+    send_ref[:, 2 * TILE :] = mm(base, dx[:, :TILE], NN).astype(BF16)
+    started = [act_copy, ship(send_ref, send_hbm, 2, w_sems.at[5])]
     for i, (part, shift) in enumerate(((low, 5), (y[:, TILE:], 2))):
         lift = ones_at((slot >= CAP) & (slot - shift < (3 if i == 0 else CAP)) & (at == slot - shift))
         tile = mm(base, part, NN) + mm(lift, dx[:, TILE:], NN)
         send_ref[:, TILE * i : TILE * i + TILE] = tile.astype(BF16)
-    send_ref[:, 2 * TILE :] = mm(base, dx[:, :TILE], NN).astype(BF16)
-    act_copy.wait()
+        started.append(ship(send_ref, send_hbm, i, w_sems.at[3 + i]))
+    for copy in started:
+        copy.wait()
 
 
 def grad_kernel(g_ref, act_ref, out_ref):
@@ -218,7 +234,6 @@
     groups = lax.axis_size("expert")
     hidden = w_up.shape[2]
     kept, padded = groups * CAP, groups * PAD
-    count = kept // 16 * 2
     shape = jax.ShapeDtypeStruct
     dma = pltpu.SemaphoreType.DMA
     tok, cot, ids, comb = tokens.T, cotangent.T, expert_ids.T, combine.T
@@ -228,26 +243,35 @@
     send, disp = call(
         dispatch_kernel,
         (shape((padded, 3 * TILE), BF16), shape((padded, 2 * toks), BF16)),
-        (VMEM, VMEM),
+        (HBM, HBM),
         (ids, comb, tok, cot),
         [HBM] * 4,
-        [pltpu.VMEM(a.shape, a.dtype) for a in (ids, comb, tok, cot)] + [dma((4,))],
+        [pltpu.VMEM(a.shape, a.dtype) for a in (ids, comb, tok, cot)]
+        + [pltpu.VMEM((padded, 3 * TILE), BF16), pltpu.VMEM((padded, 2 * toks), BF16), dma((4,)), dma((4,))],
     )
     recv = exchange(send, groups)
-    pieces = tuple(shape((16, b - a), BF16) for _ in range(kept // 16) for a, b in spans(hidden))
+    pieces = tuple(shape((r.stop - r.start, c.stop - c.start), BF16) for r, c in places(kept, hidden))
+    count = len(pieces)
     g_rows, *terms = call(
         functools.partial(up_kernel, count),
         (shape((kept, feat), BF16),) + 2 * pieces,
-        (VMEM,) + (HBM,) * (2 * count),
+        (HBM,) * (1 + 2 * count),
         (recv, up, down),
-        [VMEM, HBM, HBM],
-        [pltpu.VMEM((2, kept, hidden), BF16), *weights, dma((2,)), dma((2 * count,))],
+        [HBM] * 3,
+        [
+            pltpu.VMEM((2, kept, hidden), BF16),
+            pltpu.VMEM((padded, 3 * TILE), BF16),
+            pltpu.VMEM((kept, feat), BF16),
+            *weights,
+            dma((3,)),
+            dma((2 * count + 1,)),
+        ],
     )
     sums = lax.psum(tuple(terms), "dp")
     send_back, act = call(
         functools.partial(down_kernel, count),
         (shape((padded, 3 * TILE), BF16), shape((kept, hidden), BF16)),
-        (VMEM, HBM),
+        (HBM, HBM),
         (*sums, up, down),
         [HBM] * (2 * count + 2),
         [
@@ -256,8 +280,9 @@
             pltpu.VMEM((kept, hidden), BF16),
             pltpu.VMEM((kept, TILE), F32),
             *weights,
+            pltpu.VMEM((padded, 3 * TILE), BF16),
             dma((2 * count,)),
-            dma((3,)),
+            dma((6,)),
         ],
     )
     back = exchange(send_back, groups)

time: 161 us -> 160 us (level)
  no operation moved by 1% of the time
where the time goes in v1:
time: 160 us
  blocking collectives  113 us (71%)
  Pallas kernels  20.5 us (13%)
  starting transfers between devices  14.5 us (9%)
  waiting for transfers between devices  11.7 us (7%)
    psum x1, blocking collectives, body(): sums = lax.psum(tuple(terms), 'dp')  78.5 us
    all_to_all x1, blocking collectives, exchange(): lax.all_to_all(parts, 'expert', split_axis=0, concat_axis=0, tiled=True)  34.1 us
    pallas_call x5, Pallas kernels, call(): pl.pallas_call(kernel, out_shape=out_shape, in_specs=in_specs, out_specs=...  20.5 us
    all_to_all x1, starting transfers between devices, exchange(): lax.all_to_all(parts, 'expert', split_axis=0, concat_axis=0, tiled=True)  14.5 us
    all_to_all x1, waiting for transfers between devices, exchange(): lax.all_to_all(parts, 'expert', split_axis=0, concat_axis=0, tiled=True)  11.7 us
  transfers between devices with their start and end apart: 1, of which 1 were waited for; matrix products, arithmetic and copies ran while one was open for 0% of the time, Pallas kernels for 2%

profile of v1, /device:TPU:1, one launch (start us, length us, event | category | flops | bytes accessed | tf_op | source)
XLA Modules:
  0.0 160.0 jit_solution(12505041978127004843)
XLA Ops:
  0.6 2.3 %shard_map.93 = (bf16[512,384]{1,0:T(8,128)(2,1)}, bf16[512,256]{1,0:T(8,128)(2,1)}) custom-call(s32[2,128]{1,0:T(2,128)} %bitcast.23, f32[2,128]{1,0:T(2,128)} %bitcast.25, bf16[224,128]{1,0:T(8,128)(2,1)} %bitcast.19, bf16[224,128]{1,0:T(8,128)(2,1)} %bitcast.21), custom_call_target="tpu_custom_call" | custom-call | tf_op jit(solution)/shard_map/pallas_call | solution.py:41
  2.9 34.1 %all_to_all.10 = bf16[64,8,384]{2,1,0:T(8,128)(2,1)} all-to-all(bf16[64,8,384]{2,1,0:T(8,128)(2,1)} %bitcast.34), channel_id=1, replica_groups=mesh['dp'=16,'expert'=64] {'expert'}, dimensions={0} | all-to-all | bytes 786432 | tf_op jit(solution)/shard_map/all_to_all | solution.py:228
  37.1 5.7 %shard_map.94 = (bf16[320,224]{1,0:T(8,128)(2,1)}, bf16[16,1280]{1,0:T(8,128)(2,1)}, bf16[16,1152]{1,0:T(8,128)(2,1)}, bf16[16,1280]{1,0:T(8,128)(2,1)}, bf16[16...) custom-call(bf16[512,384]{1,0:T(8,128)(2,1)} %bitcast.31, ...), custom_call_target="tpu_custom_call" | custom-call | tf_op jit(solution)/shard_map/pallas_call | solution.py:41
  42.8 78.5 %all-reduce.2 = (bf16[16,1280]{1,0:T(8,128)(2,1)}, bf16[16,1152]{1,0:T(8,128)(2,1)}, bf16[16,1280]{1,0:T(8,128)(2,1)}, bf16[16,1152]{1,0:T(8,128)(2,1)}, bf16[16...) all-reduce(bf16[16,1280]{1,0:T(8,128)(2,1)} %get-tuple-element.93, ...), channel_id=1, replica_groups=mesh['dp'=16,'expert'=64] {'dp'}, use_global_device_ids=true, to_apply=%region_0.0 | all-reduce | flops 1556480 | bytes 6225920 | tf_op jit(solution)/shard_map/psum | solution.py:270
  121.2 8.1 %shard_map.95 = (bf16[512,384]{1,0:T(8,128)(2,1)}, bf16[320,2432]{1,0:T(8,128)(2,1)}) custom-call(bf16[16,1280]{1,0:T(8,128)(2,1)} %get-tuple-element.180.refs_0_, bf16[16,1152]{1,0:T(8,128)(2,1)} %get-tuple-element.181.refs_1_, bf16[16,1280]{1,0:T(8,128)(2,1)} %get-tuple-element.182.refs_2_, bf16[16,1152]{1,0:T(8,128)(2,1)} %get-tuple-element.183.refs_3_, ...), custom_call_target="tpu_custom_call" | custom-call | tf_op jit(solution)/shard_map/pallas_call | solution.py:41
  129.3 14.5 %all-to-all-start.1 = ((bf16[64,8,384]{2,1,0:T(8,128)(2,1)}), bf16[64,8,384]{2,1,0:T(8,128)(2,1)S(1)}, u32[]{:S(2)}, u32[]{:S(2)}) async-start(bf16[64,8,384]{2,1,0:T(8,128)(2,1)} %bitcast.33), calls=%async_computation.1 | async-start | bytes 786432 | tf_op jit(solution)/shard_map/all_to_all | solution.py:228
  143.8 0.0 copy-start
  143.8 0.0 copy-start.1
  143.8 0.0 copy-start.2
  143.8 0.0 copy-start.3
  143.9 0.0 copy-start.4
  143.9 3.3 %shard_map.97 = bf16[224,2432]{1,0:T(8,128)(2,1)} custom-call(bf16[320,224]{1,0:T(8,128)(2,1)} %get-tuple-element.178.g_ref, bf16[320,2432]{1,0:T(8,128)(2,1)} %get-tuple-element.179.act_ref), custom_call_target="tpu_custom_call" | custom-call | tf_op jit(solution)/shard_map/pallas_call | solution.py:41
  147.2 11.7 %all-to-all-done.1 = bf16[64,8,384]{2,1,0:T(8,128)(2,1)S(1)} async-done(((bf16[64,8,384]{2,1,0:T(8,128)(2,1)}), bf16[64,8,384]{2,1,0:T(8,128)(2,1)S(1)}, u32[]{:S(2)}, u32[]{:S(2)}) %all-to-all-start.1) | async-done | bytes 393248 | tf_op jit(solution)/shard_map/all_to_all | solution.py:228
  158.9 0.0 copy-done
  158.9 0.0 copy-done.1
  158.9 0.0 copy-done.2
  158.9 0.0 copy-done.3
  158.9 0.0 copy-done.4
  158.9 1.1 shard_map.96
Async XLA Ops:
  129.3 29.5 %all-to-all-start.1 = ((bf16[64,8,384]{2,1,0:T(8,128)(2,1)}), bf16[64,8,384]{2,1,0:T(8,128)(2,1)S(1)}, u32[]{:S(2)}, u32[]{:S(2)}) async-start(bf16[64,8,384]{2,1,0:T(8,128)(2,1)} %bitcast.33), calls=%async_computation.1 | async-start | bytes 786432 | tf_op jit(solution)/shard_map/all_to_all | solution.py:228
  143.8 15.1 %copy-start = (bf16[512,256]{1,0:T(8,128)(2,1)S(1)}, bf16[512,256]{1,0:T(8,128)(2,1)}, u32[]{:S(2)}) copy-start(bf16[512,256]{1,0:T(8,128)(2,1)} %get-tuple-element.174.disp_ref) | copy-start | bytes 786436
  143.8 15.1 %copy-start.1 = (bf16[128,224]{0,1:T(8,128)(2,1)S(1)}, bf16[128,224]{0,1:T(8,128)(2,1)}, u32[]{:S(2)}) copy-start(bf16[128,224]{0,1:T(8,128)(2,1)} %param.6) | copy-start | bytes 172036
  143.8 15.0 %copy-start.2 = (bf16[128,224]{0,1:T(8,128)(2,1)S(1)}, bf16[128,224]{0,1:T(8,128)(2,1)}, u32[]{:S(2)}) copy-start(bf16[128,224]{0,1:T(8,128)(2,1)} %param.7) | copy-start | bytes 172036
  143.8 15.0 %copy-start.3 = (s32[128,2]{0,1:T(2,128)S(1)}, s32[128,2]{0,1:T(2,128)}, u32[]{:S(2)}) copy-start(s32[128,2]{0,1:T(2,128)} %param.8) | copy-start | bytes 3076
  143.9 15.0 %copy-start.4 = (f32[128,2]{0,1:T(2,128)S(1)}, f32[128,2]{0,1:T(2,128)}, u32[]{:S(2)}) copy-start(f32[128,2]{0,1:T(2,128)} %param.9) | copy-start | bytes 3076

commit v2 on v1

--- a/solution.py
+++ b/solution.py
@@ -101,13 +101,12 @@
         copy.wait()
 
 
-def spans(hidden):
-    cut = (hidden // 2 + 127) // 128 * 128
-    return (0, cut), (cut, hidden)
+def chunks(hidden):
+    return [slice(at, min(at + 256, hidden)) for at in range(0, hidden, 256)]
 
 
 def places(kept, hidden):
-    return [(slice(r, r + 16), slice(*span)) for r in range(0, kept, 16) for span in spans(hidden)]
+    return [(slice(r, r + 80), c) for c in chunks(hidden) for r in range(0, kept, 80)]
 
 
 def up_kernel(count, recv_hbm, up_hbm, down_hbm, g_hbm, *refs):
@@ -129,64 +128,95 @@
     g_ref[...] = g_rows
     started = [pltpu.make_async_copy(g_ref, g_hbm, out_sems.at[2 * count])]
     started[0].start()
+    where = places(kept, hidden)
     for k, (rows, w_ref) in enumerate(((x_rows, up_ref), (g_rows, down_ref))):
         copies[k].wait()
-        for at in range(0, hidden, 256):
-            cols = slice(at, min(at + 256, hidden))
+        for cols in chunks(hidden):
             term_ref[k, :, cols] = mm(rows, w_ref[:, cols], NN).astype(BF16)
-        for i, (r, c) in enumerate(places(kept, hidden), k * count):
-            copy = pltpu.make_async_copy(term_ref.at[k, r, c], outs[i], out_sems.at[i])
-            copy.start()
-            started.append(copy)
+            for i, (r, c) in enumerate(where, k * count):
+                if c == cols:
+                    copy = pltpu.make_async_copy(term_ref.at[k, r, c], outs[i], out_sems.at[i])
+                    copy.start()
+                    started.append(copy)
     for copy in started:
         copy.wait()
 
 
 def down_kernel(count, *refs):
     sums, (up_hbm, down_hbm) = refs[: 2 * count], refs[2 * count : 2 * count + 2]
-    send_hbm, act_hbm, sum_ref, act_ref, dhid_ref, dots_ref, up_ref, down_ref, send_ref, sems, w_sems = refs[2 * count + 2 :]
+    send_hbm, act_hbm, sum_ref, act_ref, dhid_ref, dots_ref, y_ref, dx_ref, up_ref, down_ref, send_ref, sems, w_sems = refs[
+        2 * count + 2 :
+    ]
     kept, hidden = act_ref.shape
-    padded, feat = send_ref.shape[0], up_ref.shape[0]
-    half = feat // 2
-    waits = {}
-    for i, (r, c) in enumerate(places(kept, hidden)):
-        for k in range(2):
-            copy = pltpu.make_async_copy(sums[k * count + i], sum_ref.at[k, r, c], sems.at[k * count + i])
-            copy.start()
-            waits.setdefault(r.start, []).append(copy)
-    copies = load(((up_hbm, up_ref), (down_hbm, down_ref)), w_sems)
-    for first in range(0, kept, 16):
-        for copy in waits[first]:
-            copy.wait()
-        rows = slice(first, first + 16)
-        h = sum_ref[0, rows, :].astype(F32)
-        d = sum_ref[1, rows, :].astype(F32)
-        s = 1.0 / (1.0 + jnp.exp(-h))
-        act = (h * s).astype(BF16)
-        act_ref[rows, :] = act
-        dhid_ref[rows, :] = (d * (s * (1.0 + h * (1.0 - s)))).astype(BF16)
-        dots_ref[rows, :] = jnp.broadcast_to(jnp.sum(act.astype(F32) * d, axis=1, keepdims=True), (16, TILE))
-    act_copy = pltpu.make_async_copy(act_ref, act_hbm, w_sems.at[2])
-    act_copy.start()
+    padded, half = send_ref.shape[0], up_hbm.shape[0] // 2
+    where = places(kept, hidden)
+    parts = chunks(hidden)
+
+    def fetch(cols):
+        copies = []
+        for i, (r, c) in enumerate(where):
+            if c == cols:
+                for k in range(2):
+                    copy = pltpu.make_async_copy(sums[k * count + i], sum_ref.at[k, r, c], sems.at[k * count + i])
+                    copy.start()
+                    copies.append(copy)
+        return copies
+
+    waits = [fetch(parts[0])]
+    halved = [
+        (src.at[slice(half * i, half * i + half), :], dst.at[slice(TILE * i, TILE * i + half), :])
+        for src, dst in ((up_hbm, up_ref), (down_hbm, down_ref))
+        for i in range(2)
+    ]
+    copies = load(halved, w_sems)
+    waits += [fetch(cols) for cols in parts[1:]]
+    for ref in (up_ref, down_ref):
+        for i in range(2):
+            ref[TILE * i + half : TILE * i + TILE, :] = jnp.zeros((TILE - half, hidden), BF16)
+
+    def products(cols, first):
+        y = mm(act_ref[:, cols], down_ref[:, cols], NT)
+        dx = mm(dhid_ref[:, cols], up_ref[:, cols], NT)
+        y_ref[...] = y if first else y_ref[...] + y
+        dx_ref[...] = dx if first else dx_ref[...] + dx
+
+    started = []
+    for n, cols in enumerate(parts):
+        if n == 0:
+            for copy in sum(waits, []) + copies:
+                copy.wait()
+        for at in range(0, kept, 16):
+            rows = slice(at, at + 16)
+            h = sum_ref[0, rows, cols].astype(F32)
+            d = sum_ref[1, rows, cols].astype(F32)
+            s = 1.0 / (1.0 + jnp.exp(-h))
+            act = (h * s).astype(BF16)
+            act_ref[rows, cols] = act
+            dhid_ref[rows, cols] = (d * (s * (1.0 + h * (1.0 - s)))).astype(BF16)
+            dot = act.astype(F32) * d
+            dot = sum(dot[:, lane : lane + TILE] for lane in range(0, dot.shape[1], TILE))
+            dots_ref[rows, :] = dot if n == 0 else dots_ref[rows, :] + dot
+        if n > 0:
+            products(parts[n - 1], n == 1)
+    started.append(pltpu.make_async_copy(act_ref, act_hbm, w_sems.at[4]))
+    started[0].start()
+    products(parts[-1], len(parts) == 1)
     row = iota((padded, kept), 0)
     slot = row & 7
     at = iota((padded, kept), 1) - (row >> 3) * CAP
     base = ones_at((at == slot) & (slot < CAP))
-    copies[1].wait()
-    y = mm(act_ref[...], halves(down_ref[...]), NT).astype(BF16)
-    dots = dots_ref[...]
+    y, dx = y_ref[...].astype(BF16), dx_ref[...].astype(BF16)
+    dots = jnp.sum(dots_ref[...], axis=1, keepdims=True)
     high = dots.astype(BF16).astype(F32)
     lane = iota((kept, TILE), 1)
     low = jnp.where(lane == half, high, jnp.where(lane == half + 1, dots - high, y[:, :TILE].astype(F32))).astype(BF16)
-    copies[0].wait()
-    dx = mm(dhid_ref[...], halves(up_ref[...]), NT).astype(BF16)
     send_ref[:, 2 * TILE :] = mm(base, dx[:, :TILE], NN).astype(BF16)
-    started = [act_copy, ship(send_ref, send_hbm, 2, w_sems.at[5])]
+    started.append(ship(send_ref, send_hbm, 2, w_sems.at[7]))
     for i, (part, shift) in enumerate(((low, 5), (y[:, TILE:], 2))):
         lift = ones_at((slot >= CAP) & (slot - shift < (3 if i == 0 else CAP)) & (at == slot - shift))
         tile = mm(base, part, NN) + mm(lift, dx[:, TILE:], NN)
         send_ref[:, TILE * i : TILE * i + TILE] = tile.astype(BF16)
-        started.append(ship(send_ref, send_hbm, i, w_sems.at[3 + i]))
+        started.append(ship(send_ref, send_hbm, i, w_sems.at[5 + i]))
     for copy in started:
         copy.wait()
 
@@ -279,10 +309,13 @@
             pltpu.VMEM((kept, hidden), BF16),
             pltpu.VMEM((kept, hidden), BF16),
             pltpu.VMEM((kept, TILE), F32),
-            *weights,
+            pltpu.VMEM((kept, 2 * TILE), F32),
+            pltpu.VMEM((kept, 2 * TILE), F32),
+            pltpu.VMEM((2 * TILE, hidden), BF16),
+            pltpu.VMEM((2 * TILE, hidden), BF16),
             pltpu.VMEM((padded, 3 * TILE), BF16),
             dma((2 * count,)),
-            dma((6,)),
+            dma((8,)),
         ],
     )
     back = exchange(send_back, groups)

time: 160 us -> 159 us (level)
  Pallas kernels: 20.5 us -> 18.8 us
    pallas_call x5, Pallas kernels: 20.5 us -> 18.8 us  [call(): pl.pallas_call(kernel, out_shape=out_shape, in_specs=in_specs, out_specs=...]
where the time goes in v2:
time: 159 us; the launch traced here: 158 us
  blocking collectives  113 us (71%)
  Pallas kernels  18.8 us (12%)
  starting transfers between devices  14.6 us (9%)
  waiting for transfers between devices  11.7 us (7%)
    psum x1, blocking collectives, body(): sums = lax.psum(tuple(terms), 'dp')  78.4 us
    all_to_all x1, blocking collectives, exchange(): lax.all_to_all(parts, 'expert', split_axis=0, concat_axis=0, tiled=True)  34.1 us
    pallas_call x5, Pallas kernels, call(): pl.pallas_call(kernel, out_shape=out_shape, in_specs=in_specs, out_specs=...  18.8 us
    all_to_all x1, starting transfers between devices, exchange(): lax.all_to_all(parts, 'expert', split_axis=0, concat_axis=0, tiled=True)  14.6 us
    all_to_all x1, waiting for transfers between devices, exchange(): lax.all_to_all(parts, 'expert', split_axis=0, concat_axis=0, tiled=True)  11.7 us
  transfers between devices with their start and end apart: 1, of which 1 were waited for; matrix products, arithmetic and copies ran while one was open for 0% of the time, Pallas kernels for 2%

profile of v2, /device:TPU:1, one launch (start us, length us, event | category | flops | bytes accessed | tf_op | source)
XLA Modules:
  0.0 158.4 jit_solution(15964242232764726600)
XLA Ops:
  0.6 2.3 %shard_map.93 = (bf16[512,384]{1,0:T(8,128)(2,1)}, bf16[512,256]{1,0:T(8,128)(2,1)}) custom-call(s32[2,128]{1,0:T(2,128)} %bitcast.23, f32[2,128]{1,0:T(2,128)} %bitcast.25, bf16[224,128]{1,0:T(8,128)(2,1)} %bitcast.19, bf16[224,128]{1,0:T(8,128)(2,1)} %bitcast.21), custom_call_target="tpu_custom_call" | custom-call | tf_op jit(solution)/shard_map/pallas_call | solution.py:41
  2.9 34.1 %all_to_all.10 = bf16[64,8,384]{2,1,0:T(8,128)(2,1)} all-to-all(bf16[64,8,384]{2,1,0:T(8,128)(2,1)} %bitcast.34), channel_id=1, replica_groups=mesh['dp'=16,'expert'=64] {'expert'}, dimensions={0} | all-to-all | bytes 786432 | tf_op jit(solution)/shard_map/all_to_all | solution.py:258
  37.1 5.3 %shard_map.94 = (bf16[320,224]{1,0:T(8,128)(2,1)}, bf16[80,256]{1,0:T(8,128)(2,1)}, bf16[80,256]{1,0:T(8,128)(2,1)}, bf16[80,256]{1,0:T(8,128)(2,1)}, bf16[80,25...) custom-call(bf16[512,384]{1,0:T(8,128)(2,1)} %bitcast.31, ...), custom_call_target="tpu_custom_call" | custom-call | tf_op jit(solution)/shard_map/pallas_call | solution.py:41
  42.4 78.4 %all-reduce.2 = (bf16[80,256]{1,0:T(8,128)(2,1)}, bf16[80,256]{1,0:T(8,128)(2,1)}, bf16[80,256]{1,0:T(8,128)(2,1)}, bf16[80,256]{1,0:T(8,128)(2,1)}, bf16[80,256...) all-reduce(bf16[80,256]{1,0:T(8,128)(2,1)} %get-tuple-element.93, ...), channel_id=1, replica_groups=mesh['dp'=16,'expert'=64] {'dp'}, use_global_device_ids=true, to_apply=%region_0.0 | all-reduce | flops 1556480 | bytes 6225920 | tf_op jit(solution)/shard_map/psum | solution.py:300
  120.8 6.8 %shard_map.95 = (bf16[512,384]{1,0:T(8,128)(2,1)}, bf16[320,2432]{1,0:T(8,128)(2,1)}) custom-call(bf16[80,256]{1,0:T(8,128)(2,1)} %get-tuple-element.180.refs_0_, bf16[80,256]{1,0:T(8,128)(2,1)} %get-tuple-element.181.refs_1_, bf16[80,256]{1,0:T(8,128)(2,1)} %get-tuple-element.182.refs_2_, bf16[80,256]{1,0:T(8,128)(2,1)} %get-tuple-element.183.refs_3_, ...), custom_call_target="tpu_custom_call" | custom-call | tf_op jit(solution)/shard_map/pallas_call | solution.py:41
  127.6 14.6 %all-to-all-start.1 = ((bf16[64,8,384]{2,1,0:T(8,128)(2,1)}), bf16[64,8,384]{2,1,0:T(8,128)(2,1)S(1)}, u32[]{:S(2)}, u32[]{:S(2)}) async-start(bf16[64,8,384]{2,1,0:T(8,128)(2,1)} %bitcast.33), calls=%async_computation.1 | async-start | bytes 786432 | tf_op jit(solution)/shard_map/all_to_all | solution.py:258
  142.2 0.0 copy-start
  142.2 0.0 copy-start.1
  142.2 0.0 copy-start.2
  142.2 0.0 copy-start.3
  142.3 0.0 copy-start.4
  142.3 3.3 %shard_map.97 = bf16[224,2432]{1,0:T(8,128)(2,1)} custom-call(bf16[320,224]{1,0:T(8,128)(2,1)} %get-tuple-element.178.g_ref, bf16[320,2432]{1,0:T(8,128)(2,1)} %get-tuple-element.179.act_ref), custom_call_target="tpu_custom_call" | custom-call | tf_op jit(solution)/shard_map/pallas_call | solution.py:41
  145.6 11.7 %all-to-all-done.1 = bf16[64,8,384]{2,1,0:T(8,128)(2,1)S(1)} async-done(((bf16[64,8,384]{2,1,0:T(8,128)(2,1)}), bf16[64,8,384]{2,1,0:T(8,128)(2,1)S(1)}, u32[]{:S(2)}, u32[]{:S(2)}) %all-to-all-start.1) | async-done | bytes 393248 | tf_op jit(solution)/shard_map/all_to_all | solution.py:258
  157.3 0.0 copy-done
  157.3 0.0 copy-done.1
  157.3 0.0 copy-done.2
  157.3 0.0 copy-done.3
  157.3 0.0 copy-done.4
  157.3 1.1 shard_map.96
Async XLA Ops:
  127.6 29.6 %all-to-all-start.1 = ((bf16[64,8,384]{2,1,0:T(8,128)(2,1)}), bf16[64,8,384]{2,1,0:T(8,128)(2,1)S(1)}, u32[]{:S(2)}, u32[]{:S(2)}) async-start(bf16[64,8,384]{2,1,0:T(8,128)(2,1)} %bitcast.33), calls=%async_computation.1 | async-start | bytes 786432 | tf_op jit(solution)/shard_map/all_to_all | solution.py:258
  142.2 15.1 %copy-start = (bf16[512,256]{1,0:T(8,128)(2,1)S(1)}, bf16[512,256]{1,0:T(8,128)(2,1)}, u32[]{:S(2)}) copy-start(bf16[512,256]{1,0:T(8,128)(2,1)} %get-tuple-element.174.disp_ref) | copy-start | bytes 786436
  142.2 15.1 %copy-start.1 = (bf16[128,224]{0,1:T(8,128)(2,1)S(1)}, bf16[128,224]{0,1:T(8,128)(2,1)}, u32[]{:S(2)}) copy-start(bf16[128,224]{0,1:T(8,128)(2,1)} %param.6) | copy-start | bytes 172036
  142.2 15.0 %copy-start.2 = (bf16[128,224]{0,1:T(8,128)(2,1)S(1)}, bf16[128,224]{0,1:T(8,128)(2,1)}, u32[]{:S(2)}) copy-start(bf16[128,224]{0,1:T(8,128)(2,1)} %param.7) | copy-start | bytes 172036
  142.2 15.0 %copy-start.3 = (s32[128,2]{0,1:T(2,128)S(1)}, s32[128,2]{0,1:T(2,128)}, u32[]{:S(2)}) copy-start(s32[128,2]{0,1:T(2,128)} %param.8) | copy-start | bytes 3076
  142.3 15.0 %copy-start.4 = (f32[128,2]{0,1:T(2,128)S(1)}, f32[128,2]{0,1:T(2,128)}, u32[]{:S(2)}) copy-start(f32[128,2]{0,1:T(2,128)} %param.9) | copy-start | bytes 3076

commit v3 on v2

--- a/solution.py
+++ b/solution.py
@@ -111,7 +111,7 @@
 
 def up_kernel(count, recv_hbm, up_hbm, down_hbm, g_hbm, *refs):
     outs, (term_ref, recv_ref, g_ref, up_ref, down_ref, in_sems, out_sems) = refs[: 2 * count], refs[2 * count :]
-    copies = load(((up_hbm, up_ref), (down_hbm, down_ref), (recv_hbm, recv_ref)), in_sems)
+    copies = load(((recv_hbm, recv_ref), (up_hbm, up_ref), (down_hbm, down_ref)), in_sems)
     feat, hidden = up_ref.shape
     half = feat // 2
     kept, padded = g_ref.shape[0], recv_ref.shape[0]
@@ -119,7 +119,7 @@
     source = (row * 13108) >> 16
     slot = row - source * CAP
     at = iota((kept, padded), 1) - source * PAD
-    copies[2].wait()
+    copies[0].wait()
     main = mm(ones_at(at == slot), recv_ref[...], NN)
     extra = mm(ones_at(at == jnp.where(slot < 3, slot + 5, padded)), recv_ref[:, :TILE], NN)
     extra += mm(ones_at(at == jnp.where(slot < 3, padded, slot + 2)), recv_ref[:, TILE : 2 * TILE], NN)
@@ -128,9 +128,10 @@
     g_ref[...] = g_rows
     started = [pltpu.make_async_copy(g_ref, g_hbm, out_sems.at[2 * count])]
     started[0].start()
+    copies[1].wait()
+    copies[2].wait()
     where = places(kept, hidden)
     for k, (rows, w_ref) in enumerate(((x_rows, up_ref), (g_rows, down_ref))):
-        copies[k].wait()
         for cols in chunks(hidden):
             term_ref[k, :, cols] = mm(rows, w_ref[:, cols], NN).astype(BF16)
             for i, (r, c) in enumerate(where, k * count):

time: 159 us -> 158 us (level)
  no operation moved by 1% of the time
where the time goes in v3:
time: 158 us
  blocking collectives  113 us (72%)
  Pallas kernels  18 us (11%)
  starting transfers between devices  14.6 us (9%)
  waiting for transfers between devices  11.7 us (7%)
    psum x1, blocking collectives, body(): sums = lax.psum(tuple(terms), 'dp')  78.4 us
    all_to_all x1, blocking collectives, exchange(): lax.all_to_all(parts, 'expert', split_axis=0, concat_axis=0, tiled=True)  34.1 us
    pallas_call x5, Pallas kernels, call(): pl.pallas_call(kernel, out_shape=out_shape, in_specs=in_specs, out_specs=...  18 us
    all_to_all x1, starting transfers between devices, exchange(): lax.all_to_all(parts, 'expert', split_axis=0, concat_axis=0, tiled=True)  14.6 us
    all_to_all x1, waiting for transfers between devices, exchange(): lax.all_to_all(parts, 'expert', split_axis=0, concat_axis=0, tiled=True)  11.7 us
  transfers between devices with their start and end apart: 1, of which 1 were waited for; matrix products, arithmetic and copies ran while one was open for 0% of the time, Pallas kernels for 2%

profile of v3, /device:TPU:1, one launch (start us, length us, event | category | flops | bytes accessed | tf_op | source)
XLA Modules:
  0.0 157.6 jit_solution(10019004936031989658)
XLA Ops:
  0.6 2.3 %shard_map.93 = (bf16[512,384]{1,0:T(8,128)(2,1)}, bf16[512,256]{1,0:T(8,128)(2,1)}) custom-call(s32[2,128]{1,0:T(2,128)} %bitcast.23, f32[2,128]{1,0:T(2,128)} %bitcast.25, bf16[224,128]{1,0:T(8,128)(2,1)} %bitcast.19, bf16[224,128]{1,0:T(8,128)(2,1)} %bitcast.21), custom_call_target="tpu_custom_call" | custom-call | tf_op jit(solution)/shard_map/pallas_call | solution.py:41
  2.9 34.1 %all_to_all.10 = bf16[64,8,384]{2,1,0:T(8,128)(2,1)} all-to-all(bf16[64,8,384]{2,1,0:T(8,128)(2,1)} %bitcast.34), channel_id=1, replica_groups=mesh['dp'=16,'expert'=64] {'expert'}, dimensions={0} | all-to-all | bytes 786432 | tf_op jit(solution)/shard_map/all_to_all | solution.py:259
  37.1 4.5 %shard_map.94 = (bf16[320,224]{1,0:T(8,128)(2,1)}, bf16[80,256]{1,0:T(8,128)(2,1)}, bf16[80,256]{1,0:T(8,128)(2,1)}, bf16[80,256]{1,0:T(8,128)(2,1)}, bf16[80,25...) custom-call(bf16[512,384]{1,0:T(8,128)(2,1)} %bitcast.31, ...), custom_call_target="tpu_custom_call" | custom-call | tf_op jit(solution)/shard_map/pallas_call | solution.py:41
  41.6 78.4 %all-reduce.2 = (bf16[80,256]{1,0:T(8,128)(2,1)}, bf16[80,256]{1,0:T(8,128)(2,1)}, bf16[80,256]{1,0:T(8,128)(2,1)}, bf16[80,256]{1,0:T(8,128)(2,1)}, bf16[80,256...) all-reduce(bf16[80,256]{1,0:T(8,128)(2,1)} %get-tuple-element.93, ...), channel_id=1, replica_groups=mesh['dp'=16,'expert'=64] {'dp'}, use_global_device_ids=true, to_apply=%region_0.0 | all-reduce | flops 1556480 | bytes 6225920 | tf_op jit(solution)/shard_map/psum | solution.py:301
  120.0 6.8 %shard_map.95 = (bf16[512,384]{1,0:T(8,128)(2,1)}, bf16[320,2432]{1,0:T(8,128)(2,1)}) custom-call(bf16[80,256]{1,0:T(8,128)(2,1)} %get-tuple-element.180.refs_0_, bf16[80,256]{1,0:T(8,128)(2,1)} %get-tuple-element.181.refs_1_, bf16[80,256]{1,0:T(8,128)(2,1)} %get-tuple-element.182.refs_2_, bf16[80,256]{1,0:T(8,128)(2,1)} %get-tuple-element.183.refs_3_, ...), custom_call_target="tpu_custom_call" | custom-call | tf_op jit(solution)/shard_map/pallas_call | solution.py:41
  126.8 14.6 %all-to-all-start.1 = ((bf16[64,8,384]{2,1,0:T(8,128)(2,1)}), bf16[64,8,384]{2,1,0:T(8,128)(2,1)S(1)}, u32[]{:S(2)}, u32[]{:S(2)}) async-start(bf16[64,8,384]{2,1,0:T(8,128)(2,1)} %bitcast.33), calls=%async_computation.1 | async-start | bytes 786432 | tf_op jit(solution)/shard_map/all_to_all | solution.py:259
  141.4 0.0 copy-start
  141.4 0.0 copy-start.1
  141.4 0.0 copy-start.2
  141.5 0.0 copy-start.3
  141.5 0.0 copy-start.4
  141.5 3.3 %shard_map.97 = bf16[224,2432]{1,0:T(8,128)(2,1)} custom-call(bf16[320,224]{1,0:T(8,128)(2,1)} %get-tuple-element.178.g_ref, bf16[320,2432]{1,0:T(8,128)(2,1)} %get-tuple-element.179.act_ref), custom_call_target="tpu_custom_call" | custom-call | tf_op jit(solution)/shard_map/pallas_call | solution.py:41
  144.8 11.7 %all-to-all-done.1 = bf16[64,8,384]{2,1,0:T(8,128)(2,1)S(1)} async-done(((bf16[64,8,384]{2,1,0:T(8,128)(2,1)}), bf16[64,8,384]{2,1,0:T(8,128)(2,1)S(1)}, u32[]{:S(2)}, u32[]{:S(2)}) %all-to-all-start.1) | async-done | bytes 393248 | tf_op jit(solution)/shard_map/all_to_all | solution.py:259
  156.5 0.0 copy-done
  156.5 0.0 copy-done.1
  156.5 0.0 copy-done.2
  156.5 0.0 copy-done.3
  156.5 0.0 copy-done.4
  156.5 1.1 shard_map.96
Async XLA Ops:
  126.8 29.6 %all-to-all-start.1 = ((bf16[64,8,384]{2,1,0:T(8,128)(2,1)}), bf16[64,8,384]{2,1,0:T(8,128)(2,1)S(1)}, u32[]{:S(2)}, u32[]{:S(2)}) async-start(bf16[64,8,384]{2,1,0:T(8,128)(2,1)} %bitcast.33), calls=%async_computation.1 | async-start | bytes 786432 | tf_op jit(solution)/shard_map/all_to_all | solution.py:259
  141.4 15.1 %copy-start = (bf16[512,256]{1,0:T(8,128)(2,1)S(1)}, bf16[512,256]{1,0:T(8,128)(2,1)}, u32[]{:S(2)}) copy-start(bf16[512,256]{1,0:T(8,128)(2,1)} %get-tuple-element.174.disp_ref) | copy-start | bytes 786436
  141.4 15.1 %copy-start.1 = (bf16[128,224]{0,1:T(8,128)(2,1)S(1)}, bf16[128,224]{0,1:T(8,128)(2,1)}, u32[]{:S(2)}) copy-start(bf16[128,224]{0,1:T(8,128)(2,1)} %param.6) | copy-start | bytes 172036
  141.4 15.0 %copy-start.2 = (bf16[128,224]{0,1:T(8,128)(2,1)S(1)}, bf16[128,224]{0,1:T(8,128)(2,1)}, u32[]{:S(2)}) copy-start(bf16[128,224]{0,1:T(8,128)(2,1)} %param.7) | copy-start | bytes 172036
  141.5 15.0 %copy-start.3 = (s32[128,2]{0,1:T(2,128)S(1)}, s32[128,2]{0,1:T(2,128)}, u32[]{:S(2)}) copy-start(s32[128,2]{0,1:T(2,128)} %param.8) | copy-start | bytes 3076
  141.5 15.0 %copy-start.4 = (f32[128,2]{0,1:T(2,128)S(1)}, f32[128,2]{0,1:T(2,128)}, u32[]{:S(2)}) copy-start(f32[128,2]{0,1:T(2,128)} %param.9) | copy-start | bytes 3076
